TPU v7x, 512 devices: a whole 4x4x16 slice. The times are simulated.
512 devices in a mesh: dp: 32 (over z_lo, x, core), mp: 16 (over z_hi, y).
Axes of the slice: x: 4, y: 4, z: 16 (z_hi: 4, z_lo: 4; z = z_hi * 4 + z_lo), core: 2. Of those that a mesh axis runs over, the one named last changes fastest.
Arguments:
- grads: bfloat16 [32, 2, 256, 28672], P('dp', None, None, 'mp'), may hold values from -6 to 6
- weights: bfloat16 [2, 256, 28672], P(None, 'dp', 'mp'), may hold values from -1.5 to 1.5
- first_moment: float32 [2, 256, 256], P(None, 'dp'), may hold values from -6 to 6
- second_moment: float32 [2, 256, 256], P(None, 'dp'), may hold values from 1 to 16
- old_seeds: int32 [2], replicated, may hold values from 0 to 999999
- new_seeds: int32 [2], replicated, may hold values from 0 to 999999
Outputs:
- new_weights: bfloat16 [2, 256, 28672], P(None, None, 'mp')
- new_first: float32 [2, 256, 256], P(None, 'dp')
- new_second: float32 [2, 256, 256], P(None, 'dp')
Inputs may be any that keep to these rules, and one draw needn't show every extreme that they name: `old_seeds`: seeds of the counter-based generator; old and new seeds are drawn independently. `new_seeds`: seeds of the counter-based generator; old and new seeds are drawn independently.
All inputs are finite; a program needn't handle non-finite values.
Results may differ from a plain program's by a relative error of at most 0.0053.
Values may be sent and summed in bfloat16 or wider, within the bound.
No kernel may reach another device: no remote copies, remote signals or barrier semaphores. Data moves between devices by JAX's collectives and lax.ppermute only.
A program may use at most 64 MiB of HBM per device.

v0:
```python
import math
import jax
import jax.numpy as jnp
from jax import lax
from jax.sharding import PartitionSpec as P


def scramble(values):
    return (values % 46000 * (values // 2 % 46000 + 1) + 12345) % 65521


def generate(seed_value, rank_ids, columns):
    offset = seed_value % 65521
    row_key = (rank_ids * 251 + offset * 3) % 65521
    col_key = scramble((columns * 7 + offset) % 65521)
    hashed = scramble((row_key[:, None] + 2 * col_key[None, :]) % 65521)
    hashed = scramble((hashed * 3 + row_key[:, None]) % 65521)
    spread = math.sqrt(12.0 / rank_ids.shape[0])
    return ((hashed.astype(jnp.float32) + 0.5) / 65521.0 - 0.5) * spread


def inner_rank(left, right):
    return lax.dot_general(
        left, right, (((1,), (1,)), ((), ())), preferred_element_type=jnp.float32
    )


def shards(grads, weights, first_moment, second_moment, old_seeds, new_seeds):
    layers = weights.shape[0]
    rank = first_moment.shape[2]
    ncols = weights.shape[2]
    col_start = lax.axis_index("mp") * ncols
    columns = col_start + jnp.arange(ncols, dtype=jnp.int32)
    rank_ids = jnp.arange(rank, dtype=jnp.int32)
    new_projs = [
        generate(new_seeds[layer_id], rank_ids, columns).astype(jnp.bfloat16)
        for layer_id in range(layers)
    ]
    gathered = []
    firsts = []
    seconds = []
    for layer_id in range(layers):
        new_proj = new_projs[layer_id]
        old_proj = generate(old_seeds[layer_id], rank_ids, columns).astype(jnp.bfloat16)
        gram_matrix = lax.psum(inner_rank(old_proj, new_proj), "mp")
        partial_value = inner_rank(grads[0, layer_id], new_proj)
        owned = lax.psum_scatter(partial_value, "dp", scatter_dimension=0, tiled=True)
        compressed = lax.psum(owned, "mp")
        moment = (
            0.9 * jnp.dot(first_moment[layer_id], gram_matrix, precision=lax.Precision.HIGHEST)
            + 0.1 * compressed
        )
        second = (
            0.95
            * jnp.dot(
                second_moment[layer_id], gram_matrix * gram_matrix, precision=lax.Precision.HIGHEST
            )
            + 0.05 * compressed * compressed
        )
        direction = (moment / (jnp.sqrt(second) + 1e-08)).astype(jnp.bfloat16)
        update = jnp.dot(direction, new_proj, preferred_element_type=jnp.float32)
        block = (weights[layer_id].astype(jnp.float32) - 0.5 * update).astype(jnp.bfloat16)
        gathered.append(lax.all_gather(block, "dp", axis=0, tiled=True))
        firsts.append(moment)
        seconds.append(second)
    new_weights = jnp.stack(gathered)
    return (new_weights, jnp.stack(firsts), jnp.stack(seconds))


def solution(mesh):
    placed = (
        P("dp", None, None, "mp"),
        P(None, "dp", "mp"),
        P(None, "dp", None),
        P(None, "dp", None),
        P(),
        P(),
    )
    return jax.shard_map(
        shards,
        mesh=mesh,
        in_specs=placed,
        out_specs=(P(None, None, "mp"), P(None, "dp", None), P(None, "dp", None)),
        check_vma=False,
    )
```

profile of v0, /device:TPU:1, one launch (start us, length us, event | category | flops | bytes accessed | tf_op | source)
XLA Modules:
  0.0 542.0 jit_solution(2791521066732754462)
XLA Ops:
  8.0 0.0 reduce-scatter.5.cloned.1.call-start
  8.0 1.3 fusion.313
  10.1 0.0 copy-start.3
  10.1 11.9 %convolution_bitcast_fusion = f32[256,256]{1,0:T(8,128)} fusion(bf16[1,2,256,1792]{3,2,1,0:T(8,128)(2,1)} %param.6, s32[1792]{0:T(1024)S(1)} %fusion.205, s32[256]{0:T(256)S(1)} %and_select_fusion), kind=kOutput, calls=%fused_computation.211 | convolution fusion | flops 277544960 | bytes 1187840 | tf_op jit(solution)/shard_map/dot_general | solution.py:23
  22.0 0.0 reduce-scatter.5.cloned.1.call-update
  22.1 0.3 reduce-scatter.3.cloned.1.call-start
  23.1 0.0 copy-done.3
  23.1 0.0 copy-start.2
  23.1 10.6 %convolution_bitcast_fusion.1 = f32[256,256]{1,0:T(8,128)} fusion(bf16[1,2,256,1792]{3,2,1,0:T(8,128)(2,1)S(1)} %copy-done.3, s32[1792]{0:T(1024)S(1)} %fusion.191, s32[256]{0:T(256)S(1)} %and_select_fusion.2), kind=kOutput, calls=%fused_computation.212 | convolution fusion | flops 277544960 | bytes 1188864 | tf_op jit(solution)/shard_map/dot_general | solution.py:23
  33.7 0.0 reduce-scatter.3.cloned.1.call-update
  33.8 0.4 all-reduce.4.cloned.1.call-start
  34.2 0.0 copy-done.2
  34.2 0.6 fusion.312
  36.1 0.1 fusion.184
  36.2 20.4 %fusion.138 = f32[256,256]{1,0:T(8,128)} fusion(s32[1792]{0:T(1024)S(1)} %fusion.191, s32[256]{0:T(256)S(1)} %and_select_fusion.2, s32[1792]{0:T(1024)S(1)} %get-tuple-element.11, s32[256]{0:T(256)S(1)} %and_select_fusion.3), kind=kOutput, calls=%fused_computation.226 | convolution fusion | flops 320208896 | bytes 278528 | tf_op jit(solution)/shard_map/dot_general | solution.py:23
  56.7 0.0 copy-start
  56.7 0.0 copy-start.1
  56.7 0.0 copy-start.4
  56.7 20.8 %fusion.136 = f32[256,256]{1,0:T(8,128)} fusion(s32[1792]{0:T(1024)S(1)} %get-tuple-element.12, s32[256]{0:T(256)S(1)} %and_select_fusion.1, s32[1792]{0:T(1024)S(1)} %fusion.205, s32[256]{0:T(256)S(1)} %and_select_fusion), kind=kOutput, calls=%fused_computation.225 | convolution fusion | flops 320208896 | bytes 278528 | tf_op jit(solution)/shard_map/dot_general | solution.py:23
  77.5 0.0 all-reduce.4.cloned.1.call-update
  77.5 95.8 %reduce-scatter.5.cloned.1.call-done = f32[8,256]{1,0:T(8,128)} async-done(((f32[256,256]{1,0:T(8,128)}), f32[8,256]{1,0:T(8,128)}) %reduce-scatter.5.cloned.1.call-update) | async-done | bytes 8208 | tf_op jit(solution)/shard_map/reduce_scatter | solution.py:47
  173.4 149.7 %reduce-scatter.3.cloned.1.call-done = f32[8,256]{1,0:T(8,128)} async-done(((f32[256,256]{1,0:T(8,128)}), f32[8,256]{1,0:T(8,128)}) %reduce-scatter.3.cloned.1.call-update) | async-done | bytes 8208 | tf_op jit(solution)/shard_map/reduce_scatter | solution.py:47
  323.1 84.7 %all-reduce = (f32[8,256]{1,0:T(8,128)S(1)}, f32[8,256]{1,0:T(8,128)S(1)}) all-reduce(f32[8,256]{1,0:T(8,128)} %reduce-scatter.5.cloned.1.call-done, f32[8,256]{1,0:T(8,128)} %reduce-scatter.3.cloned.1.call-done), channel_id=1, replica_groups=mesh['dp'=32,'mp'=16] {'mp'}, use_global_device_ids=true, to_apply=%region_5.6 | all-reduce | flops 4096 | bytes 32768 | tf_op jit(solution)/shard_map/psum | solution.py:48
  407.8 0.0 all-reduce.4.cloned.1.call-done
  407.8 0.0 copy-done
  407.8 1.2 fusion.129
  408.9 0.0 copy-done.1
  409.0 1.2 fusion.131
  410.1 1.2 fusion.133
  411.4 1.2 fusion.135
  412.6 0.0 copy-done.4
  412.6 9.8 %fusion.3 = bf16[8,1792]{1,0:T(8,128)(2,1)S(1)} fusion(s32[1792]{0:T(1024)S(1)} %fusion.205, s32[256]{0:T(256)S(1)} %and_select_fusion, bf16[2,8,1792]{2,1,0:T(8,128)(2,1)S(1)} %copy-done.4, f32[8,256]{1,0:T(8,128)S(1)} %fusion.131, f32[8,256]{1,0:T(8,128)S(1)} %fusion.129), kind=kOutput, calls=%fused_computation.69 | convolution fusion | flops 50067456 | bytes 81920 | tf_op jit(solution)/shard_map/dot_general | solution.py:61
  422.4 57.5 %all_gather.7 = bf16[256,1792]{1,0:T(8,128)(2,1)S(1)} all-gather(bf16[8,1792]{1,0:T(8,128)(2,1)S(1)} %fusion.3), channel_id=1, replica_groups=mesh['dp'=32,'mp'=16] {'dp'}, dimensions={0}, use_global_device_ids=true | all-gather | bytes 946176 | tf_op jit(solution)/shard_map/all_gather | solution.py:63
  479.9 9.8 %fusion.2 = bf16[8,1792]{1,0:T(8,128)(2,1)S(1)} fusion(s32[1792]{0:T(1024)S(1)} %fusion.191, s32[256]{0:T(256)S(1)} %and_select_fusion.2, bf16[2,8,1792]{2,1,0:T(8,128)(2,1)S(1)} %copy-done.4, f32[8,256]{1,0:T(8,128)S(1)} %fusion.135, f32[8,256]{1,0:T(8,128)S(1)} %fusion.133), kind=kOutput, calls=%fused_computation.68 | convolution fusion | flops 50067456 | bytes 81920 | tf_op jit(solution)/shard_map/dot_general | solution.py:61
  489.7 41.9 %all_gather.6 = bf16[256,1792]{1,0:T(8,128)(2,1)S(1)} all-gather(bf16[8,1792]{1,0:T(8,128)(2,1)S(1)} %fusion.2), channel_id=1, replica_groups=mesh['dp'=32,'mp'=16] {'dp'}, dimensions={0}, use_global_device_ids=true | all-gather | bytes 946176 | tf_op jit(solution)/shard_map/all_gather | solution.py:63
  531.6 0.6 pad_maximum_fusion.2
  532.2 0.6 pad_maximum_fusion.1
  532.8 1.4 pad_maximum_fusion
  (6 shorter events, 0.2 us)
Async XLA Ops:
  8.0 165.4 %reduce-scatter.5.cloned.1.call-start = ((), (), s32[]{:S(2)}) async-start(), calls=%async_computation.3 | async-start | bytes 270336 | tf_op jit(solution)/shard_map/reduce_scatter | solution.py:47
  10.1 13.0 %copy-start.3 = (bf16[1,2,256,1792]{3,2,1,0:T(8,128)(2,1)S(1)}, bf16[1,2,256,1792]{3,2,1,0:T(8,128)(2,1)}, u32[]{:S(2)}) copy-start(bf16[1,2,256,1792]{3,2,1,0:T(8,128)(2,1)} %param.6) | copy-start | bytes 5505028
  22.1 301.0 %reduce-scatter.3.cloned.1.call-start = ((), (), s32[]{:S(2)}) async-start(), calls=%async_computation.2 | async-start | bytes 270336 | tf_op jit(solution)/shard_map/reduce_scatter | solution.py:47
  23.1 11.1 %copy-start.2 = (s32[2]{0:T(128)S(1)}, s32[2]{0:T(128)}, u32[]{:S(2)}) copy-start(s32[2]{0:T(128)} %param.10) | copy-start | bytes 28
  33.8 374.0 %all-reduce.4.cloned.1.call-start = ((), (), s32[]{:S(2)}) async-start(), calls=%async_computation.4 | async-start | bytes 1048576 | tf_op jit(solution)/shard_map/psum | solution.py:45
  56.7 351.1 %copy-start = (f32[2,8,256]{2,1,0:T(8,128)S(1)}, f32[2,8,256]{2,1,0:T(8,128)}, u32[]{:S(2)}) copy-start(f32[2,8,256]{2,1,0:T(8,128)} %param.9) | copy-start | bytes 49156
  56.7 352.3 %copy-start.1 = (f32[2,8,256]{2,1,0:T(8,128)S(1)}, f32[2,8,256]{2,1,0:T(8,128)}, u32[]{:S(2)}) copy-start(f32[2,8,256]{2,1,0:T(8,128)} %param.8) | copy-start | bytes 49156
  56.7 355.9 %copy-start.4 = (bf16[2,8,1792]{2,1,0:T(8,128)(2,1)S(1)}, bf16[2,8,1792]{2,1,0:T(8,128)(2,1)}, u32[]{:S(2)}) copy-start(bf16[2,8,1792]{2,1,0:T(8,128)(2,1)} %param.7) | copy-start | bytes 172036
Sparse Core Ops, SparseCore 0:
  22.2 151.1 reduce-scatter.4
  176.1 146.8 reduce-scatter.2
Sparse Core Ops, SparseCore 1:
  77.6 199.6 all-reduce.3
where the time goes:
time: 550 us; the launch traced here: 542 us
  waiting for transfers between devices  246 us (45%)
  blocking collectives  184 us (33%)
  matrix products  88.2 us (16%)
  between operations  18.6 us (3%)
    reduce_scatter x2, waiting for transfers between devices, shards(): lax.psum_scatter(partial_value, 'dp', scatter_dimension=0, tiled=True)  246 us
    all_gather x2, blocking collectives, shards(): gathered.append(lax.all_gather(block, 'dp', axis=0, tiled=True))  99.4 us
    psum x1, blocking collectives, shards(): compressed = lax.psum(owned, 'mp')  84.7 us
    dot_general x4, matrix products, inner_rank(): lax.dot_general(left, right, (((1,), (1,)), ((), ())), preferred_element_...  63.8 us
    dot_general x2, matrix products, shards(): update = jnp.dot(direction, new_proj, preferred_element_type=jnp.float32)  19.6 us
  transfers between devices with their start and end apart: 3, of which 2 were waited for; matrix products, arithmetic and copies ran while one was open for 10% of the time, Pallas kernels for 0%

commit v1 on v0

--- a/solution.py
+++ b/solution.py
@@ -45,7 +45,8 @@
         gram_matrix = lax.psum(inner_rank(old_proj, new_proj), "mp")
         partial_value = inner_rank(grads[0, layer_id], new_proj)
         owned = lax.psum_scatter(partial_value, "dp", scatter_dimension=0, tiled=True)
-        compressed = lax.psum(owned, "mp")
+        tmp = lax.all_gather(owned, "mp")
+        compressed = jnp.sum(tmp, 0)
         moment = (
             0.9 * jnp.dot(first_moment[layer_id], gram_matrix, precision=lax.Precision.HIGHEST)
             + 0.1 * compressed

time: 550 us -> 505 us (0.918)
  waiting for transfers between devices: 246 us -> 197 us
    all_gather x0 -> x2, blocking collectives: none -> 94.5 us  [shards(): tmp = lax.all_gather(owned, 'mp')]
    reduce_scatter x2, waiting for transfers between devices: 246 us -> 154 us  [shards(): lax.psum_scatter(partial_value, 'dp', scatter_dimension=0, tiled=True)]
    psum x1 -> x0, blocking collectives: 84.7 us -> none  [shards(): compressed = lax.psum(owned, 'mp')]
    psum x1, waiting for transfers between devices: 0.01 us -> 43 us  [shards(): gram_matrix = lax.psum(inner_rank(old_proj, new_proj), 'mp')]
    all_gather x2, blocking collectives: 99.4 us -> 92.8 us  [shards(): gathered.append(lax.all_gather(block, 'dp', axis=0, tiled=True))]
  transfers between devices with their start and end apart: 3 -> 3, of which waited for: 2 -> 3; matrix products, arithmetic and copies ran while one was open for 10% -> 11% of each run, Pallas kernels for 0% -> 0%
where the time goes in v1:
time: 505 us; the launch traced here: 497 us
  waiting for transfers between devices  197 us (39%)
  blocking collectives  187 us (37%)
  matrix products  86.6 us (17%)
  between operations  18.5 us (4%)
    reduce_scatter x2, waiting for transfers between devices, shards(): lax.psum_scatter(partial_value, 'dp', scatter_dimension=0, tiled=True)  154 us
    all_gather x2, blocking collectives, shards(): tmp = lax.all_gather(owned, 'mp')  94.5 us
    all_gather x2, blocking collectives, shards(): gathered.append(lax.all_gather(block, 'dp', axis=0, tiled=True))  92.8 us
    dot_general x4, matrix products, inner_rank(): lax.dot_general(left, right, (((1,), (1,)), ((), ())), preferred_element_...  62.3 us
    psum x1, waiting for transfers between devices, shards(): gram_matrix = lax.psum(inner_rank(old_proj, new_proj), 'mp')  43 us
    dot_general x2, matrix products, shards(): update = jnp.dot(direction, new_proj, preferred_element_type=jnp.float32)  19.6 us
  transfers between devices with their start and end apart: 3, of which 3 were waited for; matrix products, arithmetic and copies ran while one was open for 11% of the time, Pallas kernels for 0%

profile of v1, /device:TPU:1, one launch (start us, length us, event | category | flops | bytes accessed | tf_op | source)
XLA Modules:
  0.0 497.0 jit_solution(18124603267146385812)
XLA Ops:
  8.0 0.0 reduce-scatter.9.cloned.1.call-start
  8.0 1.3 fusion.312
  10.0 1.4 fusion.313
  12.1 0.1 fusion.198
  12.2 11.1 %convolution_bitcast_fusion = f32[256,256]{0,1:T(8,128)S(1)} fusion(bf16[1,2,256,1792]{3,2,1,0:T(8,128)(2,1)} %param.6, s32[1792]{0:T(1024)S(1)} %get-tuple-element.12, s32[256]{0:T(256)S(1)} %get-tuple-element.13), kind=kOutput, calls=%fused_computation.211 | convolution fusion | flops 277544960 | bytes 1187840 | tf_op jit(solution)/shard_map/dot_general | solution.py:23
  23.3 0.8 copy.15
  24.1 0.0 reduce-scatter.9.cloned.1.call-update
  24.2 0.2 all-reduce.3.cloned.1.call-start
  25.7 0.1 fusion.184
  25.8 20.5 %fusion.136 = f32[256,256]{1,0:T(8,128)} fusion(s32[1792]{0:T(1024)S(1)} %get-tuple-element.11, s32[256]{0:T(256)S(1)} %get-tuple-element.14, s32[1792]{0:T(1024)S(1)} %get-tuple-element.12, s32[256]{0:T(256)S(1)} %get-tuple-element.13), kind=kOutput, calls=%fused_computation.225 | convolution fusion | flops 320208896 | bytes 278528 | tf_op jit(solution)/shard_map/dot_general | solution.py:23
  46.3 0.0 copy-start.2
  46.3 20.9 %fusion.138 = f32[256,256]{1,0:T(8,128)} fusion(s32[1792]{0:T(1024)S(1)} %get-tuple-element.10, s32[256]{0:T(256)S(1)} %get-tuple-element.15, s32[1792]{0:T(1024)S(1)} %get-tuple-element.9, s32[256]{0:T(256)S(1)} %get-tuple-element.16), kind=kOutput, calls=%fused_computation.226 | convolution fusion | flops 320208896 | bytes 278528 | tf_op jit(solution)/shard_map/dot_general | solution.py:23
  67.2 0.0 all-reduce.3.cloned.1.call-update
  67.2 0.0 copy-start
  67.2 0.0 copy-start.1
  67.2 0.0 reduce-scatter.7.cloned.1.call-start
  67.3 0.0 copy-done.2
  67.3 9.9 %convolution_bitcast_fusion.1 = f32[256,256]{0,1:T(8,128)S(1)} fusion(bf16[1,2,256,1792]{3,2,1,0:T(8,128)(2,1)S(1)} %copy-done.2, s32[1792]{0:T(1024)S(1)} %get-tuple-element.10, s32[256]{0:T(256)S(1)} %get-tuple-element.15), kind=kOutput, calls=%fused_computation.212 | convolution fusion | flops 277544960 | bytes 1188864 | tf_op jit(solution)/shard_map/dot_general | solution.py:23
  77.2 0.0 copy-start.3
  77.2 0.8 copy.13
  78.0 0.0 reduce-scatter.7.cloned.1.call-update
  78.1 97.5 %reduce-scatter.9.cloned.1.call-done = f32[8,256]{1,0:T(8,128)} async-done(((f32[256,256]{1,0:T(8,128)}), f32[8,256]{1,0:T(8,128)}) %reduce-scatter.9.cloned.1.call-update) | async-done | bytes 8208 | tf_op jit(solution)/shard_map/reduce_scatter | solution.py:47
  175.6 48.2 %all-gather.1 = f32[128,256]{1,0:T(8,128)S(1)} all-gather(f32[8,256]{1,0:T(8,128)} %reduce-scatter.9.cloned.1.call-done), channel_id=3, replica_groups=mesh['dp'=32,'mp'=16] {'mp'}, dimensions={0}, use_global_device_ids=true | all-gather | bytes 139264 | tf_op jit(solution)/shard_map/all_gather | solution.py:48
  223.8 43.0 %all-reduce.3.cloned.1.call-done = (f32[256,256]{1,0:T(8,128)}, f32[256,256]{1,0:T(8,128)}) async-done(((f32[256,256]{1,0:T(8,128)}, f32[256,256]{1,0:T(8,128)}), (f32[256,256]{1,0:T(8,128)}, f32[256,256]{1,0:T(8,128)})) %all-reduce.3.cloned.1.call-update) | async-done | bytes 524304 | tf_op jit(solution)/shard_map/psum | solution.py:45
  266.8 0.0 copy-done
  266.8 1.2 fusion.129
  268.0 0.0 copy-done.1
  268.0 1.2 fusion.131
  269.2 56.3 %reduce-scatter.7.cloned.1.call-done = f32[8,256]{1,0:T(8,128)} async-done(((f32[256,256]{1,0:T(8,128)}), f32[8,256]{1,0:T(8,128)}) %reduce-scatter.7.cloned.1.call-update) | async-done | bytes 8208 | tf_op jit(solution)/shard_map/reduce_scatter | solution.py:47
  325.5 46.3 %all-gather = f32[128,256]{1,0:T(8,128)S(1)} all-gather(f32[8,256]{1,0:T(8,128)} %reduce-scatter.7.cloned.1.call-done), channel_id=2, replica_groups=mesh['dp'=32,'mp'=16] {'mp'}, dimensions={0}, use_global_device_ids=true | all-gather | bytes 139264 | tf_op jit(solution)/shard_map/all_gather | solution.py:48
  371.9 1.2 fusion.133
  373.1 1.2 fusion.135
  374.3 0.0 copy-done.3
  374.3 9.8 %fusion.2 = bf16[8,1792]{1,0:T(8,128)(2,1)S(1)} fusion(s32[1792]{0:T(1024)S(1)} %get-tuple-element.10, s32[256]{0:T(256)S(1)} %get-tuple-element.15, bf16[2,8,1792]{2,1,0:T(8,128)(2,1)S(1)} %copy-done.3, f32[8,256]{1,0:T(8,128)S(1)} %fusion.135, f32[8,256]{1,0:T(8,128)S(1)} %fusion.133), kind=kOutput, calls=%fused_computation.68 | convolution fusion | flops 50067456 | bytes 81920 | tf_op jit(solution)/shard_map/dot_general | solution.py:62
  384.1 50.9 %all_gather.20 = bf16[256,1792]{1,0:T(8,128)(2,1)S(1)} all-gather(bf16[8,1792]{1,0:T(8,128)(2,1)S(1)} %fusion.2), channel_id=1, replica_groups=mesh['dp'=32,'mp'=16] {'dp'}, dimensions={0}, use_global_device_ids=true | all-gather | bytes 946176 | tf_op jit(solution)/shard_map/all_gather | solution.py:64
  435.1 9.8 %fusion.3 = bf16[8,1792]{1,0:T(8,128)(2,1)S(1)} fusion(s32[1792]{0:T(1024)S(1)} %get-tuple-element.12, s32[256]{0:T(256)S(1)} %get-tuple-element.13, bf16[2,8,1792]{2,1,0:T(8,128)(2,1)S(1)} %copy-done.3, f32[8,256]{1,0:T(8,128)S(1)} %fusion.131, f32[8,256]{1,0:T(8,128)S(1)} %fusion.129), kind=kOutput, calls=%fused_computation.69 | convolution fusion | flops 50067456 | bytes 81920 | tf_op jit(solution)/shard_map/dot_general | solution.py:62
  444.9 41.9 %all_gather.23 = bf16[256,1792]{1,0:T(8,128)(2,1)S(1)} all-gather(bf16[8,1792]{1,0:T(8,128)(2,1)S(1)} %fusion.3), channel_id=1, replica_groups=mesh['dp'=32,'mp'=16] {'dp'}, dimensions={0}, use_global_device_ids=true | all-gather | bytes 946176 | tf_op jit(solution)/shard_map/all_gather | solution.py:64
  486.8 0.6 pad_maximum_fusion.2
  487.4 0.6 pad_maximum_fusion.1
  488.0 1.4 pad_maximum_fusion
  (4 shorter events, 0.1 us)
Async XLA Ops:
  8.0 167.6 %reduce-scatter.9.cloned.1.call-start = ((), (), s32[]{:S(2)}) async-start(), calls=%async_computation.3 | async-start | bytes 270336 | tf_op jit(solution)/shard_map/reduce_scatter | solution.py:47
  24.2 242.6 %all-reduce.3.cloned.1.call-start = ((), (), s32[]{:S(2)}) async-start(), calls=%async_computation.4 | async-start | bytes 1048576 | tf_op jit(solution)/shard_map/psum | solution.py:45
  46.3 21.0 %copy-start.2 = (bf16[1,2,256,1792]{3,2,1,0:T(8,128)(2,1)S(1)}, bf16[1,2,256,1792]{3,2,1,0:T(8,128)(2,1)}, u32[]{:S(2)}) copy-start(bf16[1,2,256,1792]{3,2,1,0:T(8,128)(2,1)} %param.6) | copy-start | bytes 5505028
  67.2 199.6 %copy-start = (f32[2,8,256]{2,1,0:T(8,128)S(1)}, f32[2,8,256]{2,1,0:T(8,128)}, u32[]{:S(2)}) copy-start(f32[2,8,256]{2,1,0:T(8,128)} %param.9) | copy-start | bytes 49156
  67.2 200.8 %copy-start.1 = (f32[2,8,256]{2,1,0:T(8,128)S(1)}, f32[2,8,256]{2,1,0:T(8,128)}, u32[]{:S(2)}) copy-start(f32[2,8,256]{2,1,0:T(8,128)} %param.8) | copy-start | bytes 49156
  67.2 258.3 %reduce-scatter.7.cloned.1.call-start = ((), (), s32[]{:S(2)}) async-start(), calls=%async_computation.2 | async-start | bytes 270336 | tf_op jit(solution)/shard_map/reduce_scatter | solution.py:47
  77.2 297.1 %copy-start.3 = (bf16[2,8,1792]{2,1,0:T(8,128)(2,1)S(1)}, bf16[2,8,1792]{2,1,0:T(8,128)(2,1)}, u32[]{:S(2)}) copy-start(bf16[2,8,1792]{2,1,0:T(8,128)(2,1)} %param.7) | copy-start | bytes 172036
Sparse Core Ops, SparseCore 0:
  24.3 151.2 reduce-scatter.8
  178.4 147.1 reduce-scatter.6
Sparse Core Ops, SparseCore 1:
  67.3 199.5 all-reduce.2
